TPU v7x, 128 devices: a whole 4x4x4 slice. The times are simulated.
128 devices in a mesh: lon: 8 (over y, core), lat: 16 (over z, x).
Axes of the slice: x: 4, y: 4, z: 4, core: 2. Of those that a mesh axis runs over, the one named last changes fastest.
Arguments:
- state: float32 [512, 4, 16, 2880], P('lat', None, None, 'lon'), may hold values from -6 to 6
- band: int32 [256], replicated, may hold values from 1 to 32, as said below
- damping: float32 [256], replicated, may hold values from 0.2 to 0.9
Outputs:
- advanced: float32 [512, 4, 16, 2880], P('lat', None, None, 'lon')
Inputs may be any that keep to these rules, and one draw needn't show every extreme that they name: Each polar latitude's band half width is an integer from 1 to 32; 32 is reached at some latitude.
All inputs are finite; a program needn't handle non-finite values.
Results may differ from a plain program's by a relative error of at most 0.00007.
Values sent between devices are 32-bit elements; how exact they have to be, the bound alone decides.
A program may use at most 128 MiB of HBM per device.

v0:
```python
import math

import jax
import jax.numpy as jnp
from jax import lax
from jax.sharding import PartitionSpec as P

MAXB = 32


KX = 0.004
KY = 0.1
FC = 0.2
GROUP = 5


def with_halo(cells, sides, width, closed):
    for axis, dim in sides:
        count = lax.axis_size(axis)
        ends = count if closed else count - 1
        head = lax.slice_in_dim(cells, 0, width, axis=dim)
        tail = lax.slice_in_dim(cells, cells.shape[dim] - width, cells.shape[dim], axis=dim)
        cells = jnp.concatenate(
            [
                lax.ppermute(tail, axis, [(i, (i + 1) % count) for i in range(ends)]),
                cells,
                lax.ppermute(head, axis, [((i + 1) % count, i) for i in range(ends)]),
            ],
            axis=dim,
        )
    return cells


def advance_cells(padded, cos_rows, sin_rows, cos_pad):
    u = padded[:, 0]
    v = padded[:, 1]
    h = padded[:, 2]
    q = padded[:, 3]
    inv = 1.0 / cos_rows[:, None, None]
    sn = sin_rows[:, None, None]
    cp = cos_pad[:, None, None]

    def middle(a):
        return a[1:-1, :, 1:-1]

    def east(a):
        return a[1:-1, :, 2:]

    def west(a):
        return a[1:-1, :, :-2]

    def north(a):
        return a[2:, :, 1:-1]

    def south(a):
        return a[:-2, :, 1:-1]

    flux_x = u * h
    flux_y = v * h * cp
    h_new = (
        middle(h)
        - KX * inv * (east(flux_x) - west(flux_x))
        - KY * inv * (north(flux_y) - south(flux_y))
    )
    u_new = middle(u) - KX * inv * (east(h) - west(h)) + FC * sn * middle(v)
    v_new = middle(v) - KY * (north(h) - south(h)) - FC * sn * middle(u)
    q_new = (
        middle(q)
        - KX * inv * middle(u) * (east(q) - west(q))
        - KY * middle(v) * (north(q) - south(q))
    )
    return jnp.stack([u_new, v_new, h_new, q_new], axis=1)


def tap_smooth(extended, width, length):
    taps = jnp.arange(-MAXB, MAXB + 1).astype(jnp.float32)
    weights = (
        jnp.maximum(width[:, None] + 1.0 - jnp.abs(taps)[None, :], 0.0)
        / (width[:, None] + 1.0) ** 2
    )
    start_shape = extended.shape[:3] + (length,)
    tap_count = 2 * MAXB + 1
    turns = tap_count // GROUP

    def add_one(tap, total):
        weight = lax.dynamic_index_in_dim(weights, tap, 1, keepdims=False)
        return total + weight[:, None, None, None] * lax.dynamic_slice_in_dim(
            extended, tap, length, 3
        )

    def add_group(step, total):
        for offset in range(GROUP):
            total = add_one(step * GROUP + offset, total)
        return total

    total = lax.fori_loop(0, turns, add_group, jnp.zeros(start_shape, jnp.float32))
    return total


def shards(state, band, damping):
    lon_count = lax.axis_size("lon")
    lat_count = lax.axis_size("lat")
    lat_rows, field_count, levels, lon_cells = state.shape
    lon_total = lon_cells * lon_count
    lat_total = lat_rows * lat_count
    polar_total = lat_total // 2
    quarter = lat_total // 4
    lon_place = lax.axis_index("lon")
    lat_place = lax.axis_index("lat")
    rimmed = with_halo(state, (("lon", 3),), 1, True)
    padded = with_halo(rimmed, (("lat", 0),), 1, False)
    rows = lat_place * lat_rows + jnp.arange(-1, lat_rows + 1, dtype=jnp.int32)
    angle = math.pi * ((rows.astype(jnp.float32) + 0.5) / lat_total - 0.5)
    cos_pad = jnp.cos(angle)
    stepped = advance_cells(padded, cos_pad[1:-1], jnp.sin(angle[1:-1]), cos_pad)
    band_float = band.astype(jnp.float32)

    def row_params(lats):
        is_polar = (lats < quarter) | (lats >= 3 * quarter)
        polar_place = jnp.where(lats < quarter, lats, lats - polar_total)
        onehot = (
            (polar_place[:, None] == jnp.arange(polar_total, dtype=jnp.int32)[None, :])
            & is_polar[:, None]
        ).astype(jnp.float32)
        width = jnp.dot(onehot, band_float, precision=lax.Precision.HIGHEST)
        strength = jnp.dot(onehot, damping, precision=lax.Precision.HIGHEST)
        return (width, strength)

    def damp_block(fields, lats):
        width, strength = row_params(lats)
        extended = jnp.concatenate([fields[..., -MAXB:], fields, fields[..., :MAXB]], axis=3)
        smooth = tap_smooth(extended, width, lon_total)
        return fields + strength[:, None, None, None] * (smooth - fields)

    gathered = lax.all_to_all(stepped, "lon", split_axis=0, concat_axis=3, tiled=True)
    part_rows = gathered.shape[0]
    spread = lax.all_to_all(gathered, "lat", split_axis=2, concat_axis=0, tiled=True)
    slots = jnp.arange(lat_count * part_rows, dtype=jnp.int32)
    lats = slots // part_rows * lat_rows + lon_place * part_rows + slots % part_rows
    edge = lat_count // 4 * part_rows
    southern = damp_block(spread[:edge], lats[:edge])
    northern = damp_block(spread[-edge:], lats[-edge:])
    spread = jnp.concatenate([southern, spread[edge:-edge], northern], axis=0)
    damped = lax.all_to_all(spread, "lat", split_axis=0, concat_axis=2, tiled=True)
    return lax.all_to_all(damped, "lon", split_axis=3, concat_axis=0, tiled=True)


def solution(mesh):
    in_specs = (P("lat", None, None, "lon"), P(), P())
    out_specs = P("lat", None, None, "lon")
    return jax.shard_map(shards, mesh=mesh, in_specs=in_specs, out_specs=out_specs, check_vma=False)
```

profile of v0, /device:TPU:1, one launch (start us, length us, event | category | flops | bytes accessed | tf_op | source)
XLA Modules:
  0.0 553.1 jit_solution(18015981450221543756)
XLA Ops:
  29.0 45.6 %all_to_all.69 = f32[32,4,16,360]{3,2,1,0:T(8,128)S(1)} all-to-all(f32[32,4,16,360]{3,2,1,0:T(8,128)S(1)} %pad_maximum_fusion.1), channel_id=1, replica_groups=mesh['lon'=8,'lat'=16] {'lon'}, dimensions={0} | all-to-all | bytes 5898240 | tf_op jit(solution)/shard_map/all_to_all | solution.py:135
  83.1 9.7 %all-to-all-start.1 = ((f32[4,4,16,2880]{3,1,0,2:T(4,128)}), f32[4,4,16,2880]{3,1,0,2:T(4,128)}, u32[]{:S(2)}, u32[]{:S(2)}) async-start(f32[4,4,16,2880]{3,1,0,2:T(4,128)} %copy.80), calls=%async_computation.1 | async-start | bytes 6029312 | tf_op jit(solution)/shard_map/all_to_all | solution.py:137
  94.0 42.7 %all-to-all-done.1 = f32[4,4,16,2880]{3,1,0,2:T(4,128)} async-done(((f32[4,4,16,2880]{3,1,0,2:T(4,128)}), f32[4,4,16,2880]{3,1,0,2:T(4,128)}, u32[]{:S(2)}, u32[]{:S(2)}) %all-to-all-start.1) | async-done | bytes 2949152 | tf_op jit(solution)/shard_map/all_to_all | solution.py:137
  145.2 115.6 %while.32 = (s32[]{:T(128)}, f32[16,4,1,2880]{3,2,1,0:T(1,128)S(1)}, f32[16,65]{0,1:T(8,128)S(1)}, f32[16,4,1,2944]{3,2,1,0:T(1,128)S(1)}, s32[]{:T(128)}, /*ind...) while((s32[]{:T(128)}, ...), condition=%wide.region_1.2_spmd.clone, body=%wide.region_0.1_spmd.clone.sunk | while | flops 2027553 | bytes 5162514 | solution.py:96
  145.3 8.8 %multiply_add_fusion.4 = f32[16,4,1,2880]{3,2,1,0:T(1,128)S(1)} fusion(f32[16,4,1,2944]{3,2,1,0:T(1,128)S(1)} %get-tuple-element.535, s32[]{:T(128)S(6)} %select_n.276, s32[]{:T(128)S(6)} %select_n.277, s32[]{:T(128)S(6)} %select_n.278, s32[]{:T(128)S(6)} %select_n.279, s32[]{:T(128)S(6)} %select_n.280, f32[16,4,1,2880]{3,2,1,0:T(1,128)S(1)} %get-tuple-element.513, ...), kind=kLoop, calls=%fused_computation.4.clone.1 | loop fusion | flops 2027520 | bytes 5161301 | tf_op jit(solution)/shard_map/while/body/eval_jaxpr/add | solution.py:87
  154.1 8.8 %multiply_add_fusion.4 = f32[16,4,1,2880]{3,2,1,0:T(1,128)S(1)} fusion(f32[16,4,1,2944]{3,2,1,0:T(1,128)S(1)} %get-tuple-element.535, s32[]{:T(128)S(6)} %select_n.276, s32[]{:T(128)S(6)} %select_n.277, s32[]{:T(128)S(6)} %select_n.278, s32[]{:T(128)S(6)} %select_n.279, s32[]{:T(128)S(6)} %select_n.280, f32[16,4,1,2880]{3,2,1,0:T(1,128)S(1)} %get-tuple-element.513, ...), kind=kLoop, calls=%fused_computation.4.clone.1 | loop fusion | flops 2027520 | bytes 5161301 | tf_op jit(solution)/shard_map/while/body/eval_jaxpr/add | solution.py:87
  163.0 8.8 %multiply_add_fusion.4 = f32[16,4,1,2880]{3,2,1,0:T(1,128)S(1)} fusion(f32[16,4,1,2944]{3,2,1,0:T(1,128)S(1)} %get-tuple-element.535, s32[]{:T(128)S(6)} %select_n.276, s32[]{:T(128)S(6)} %select_n.277, s32[]{:T(128)S(6)} %select_n.278, s32[]{:T(128)S(6)} %select_n.279, s32[]{:T(128)S(6)} %select_n.280, f32[16,4,1,2880]{3,2,1,0:T(1,128)S(1)} %get-tuple-element.513, ...), kind=kLoop, calls=%fused_computation.4.clone.1 | loop fusion | flops 2027520 | bytes 5161301 | tf_op jit(solution)/shard_map/while/body/eval_jaxpr/add | solution.py:87
  171.9 8.8 %multiply_add_fusion.4 = f32[16,4,1,2880]{3,2,1,0:T(1,128)S(1)} fusion(f32[16,4,1,2944]{3,2,1,0:T(1,128)S(1)} %get-tuple-element.535, s32[]{:T(128)S(6)} %select_n.276, s32[]{:T(128)S(6)} %select_n.277, s32[]{:T(128)S(6)} %select_n.278, s32[]{:T(128)S(6)} %select_n.279, s32[]{:T(128)S(6)} %select_n.280, f32[16,4,1,2880]{3,2,1,0:T(1,128)S(1)} %get-tuple-element.513, ...), kind=kLoop, calls=%fused_computation.4.clone.1 | loop fusion | flops 2027520 | bytes 5161301 | tf_op jit(solution)/shard_map/while/body/eval_jaxpr/add | solution.py:87
  180.8 8.8 %multiply_add_fusion.4 = f32[16,4,1,2880]{3,2,1,0:T(1,128)S(1)} fusion(f32[16,4,1,2944]{3,2,1,0:T(1,128)S(1)} %get-tuple-element.535, s32[]{:T(128)S(6)} %select_n.276, s32[]{:T(128)S(6)} %select_n.277, s32[]{:T(128)S(6)} %select_n.278, s32[]{:T(128)S(6)} %select_n.279, s32[]{:T(128)S(6)} %select_n.280, f32[16,4,1,2880]{3,2,1,0:T(1,128)S(1)} %get-tuple-element.513, ...), kind=kLoop, calls=%fused_computation.4.clone.1 | loop fusion | flops 2027520 | bytes 5161301 | tf_op jit(solution)/shard_map/while/body/eval_jaxpr/add | solution.py:87
  189.7 8.8 %multiply_add_fusion.4 = f32[16,4,1,2880]{3,2,1,0:T(1,128)S(1)} fusion(f32[16,4,1,2944]{3,2,1,0:T(1,128)S(1)} %get-tuple-element.535, s32[]{:T(128)S(6)} %select_n.276, s32[]{:T(128)S(6)} %select_n.277, s32[]{:T(128)S(6)} %select_n.278, s32[]{:T(128)S(6)} %select_n.279, s32[]{:T(128)S(6)} %select_n.280, f32[16,4,1,2880]{3,2,1,0:T(1,128)S(1)} %get-tuple-element.513, ...), kind=kLoop, calls=%fused_computation.4.clone.1 | loop fusion | flops 2027520 | bytes 5161301 | tf_op jit(solution)/shard_map/while/body/eval_jaxpr/add | solution.py:87
  198.6 8.8 %multiply_add_fusion.4 = f32[16,4,1,2880]{3,2,1,0:T(1,128)S(1)} fusion(f32[16,4,1,2944]{3,2,1,0:T(1,128)S(1)} %get-tuple-element.535, s32[]{:T(128)S(6)} %select_n.276, s32[]{:T(128)S(6)} %select_n.277, s32[]{:T(128)S(6)} %select_n.278, s32[]{:T(128)S(6)} %select_n.279, s32[]{:T(128)S(6)} %select_n.280, f32[16,4,1,2880]{3,2,1,0:T(1,128)S(1)} %get-tuple-element.513, ...), kind=kLoop, calls=%fused_computation.4.clone.1 | loop fusion | flops 2027520 | bytes 5161301 | tf_op jit(solution)/shard_map/while/body/eval_jaxpr/add | solution.py:87
  207.5 8.8 %multiply_add_fusion.4 = f32[16,4,1,2880]{3,2,1,0:T(1,128)S(1)} fusion(f32[16,4,1,2944]{3,2,1,0:T(1,128)S(1)} %get-tuple-element.535, s32[]{:T(128)S(6)} %select_n.276, s32[]{:T(128)S(6)} %select_n.277, s32[]{:T(128)S(6)} %select_n.278, s32[]{:T(128)S(6)} %select_n.279, s32[]{:T(128)S(6)} %select_n.280, f32[16,4,1,2880]{3,2,1,0:T(1,128)S(1)} %get-tuple-element.513, ...), kind=kLoop, calls=%fused_computation.4.clone.1 | loop fusion | flops 2027520 | bytes 5161301 | tf_op jit(solution)/shard_map/while/body/eval_jaxpr/add | solution.py:87
  216.4 8.8 %multiply_add_fusion.4 = f32[16,4,1,2880]{3,2,1,0:T(1,128)S(1)} fusion(f32[16,4,1,2944]{3,2,1,0:T(1,128)S(1)} %get-tuple-element.535, s32[]{:T(128)S(6)} %select_n.276, s32[]{:T(128)S(6)} %select_n.277, s32[]{:T(128)S(6)} %select_n.278, s32[]{:T(128)S(6)} %select_n.279, s32[]{:T(128)S(6)} %select_n.280, f32[16,4,1,2880]{3,2,1,0:T(1,128)S(1)} %get-tuple-element.513, ...), kind=kLoop, calls=%fused_computation.4.clone.1 | loop fusion | flops 2027520 | bytes 5161301 | tf_op jit(solution)/shard_map/while/body/eval_jaxpr/add | solution.py:87
  225.3 8.8 %multiply_add_fusion.4 = f32[16,4,1,2880]{3,2,1,0:T(1,128)S(1)} fusion(f32[16,4,1,2944]{3,2,1,0:T(1,128)S(1)} %get-tuple-element.535, s32[]{:T(128)S(6)} %select_n.276, s32[]{:T(128)S(6)} %select_n.277, s32[]{:T(128)S(6)} %select_n.278, s32[]{:T(128)S(6)} %select_n.279, s32[]{:T(128)S(6)} %select_n.280, f32[16,4,1,2880]{3,2,1,0:T(1,128)S(1)} %get-tuple-element.513, ...), kind=kLoop, calls=%fused_computation.4.clone.1 | loop fusion | flops 2027520 | bytes 5161301 | tf_op jit(solution)/shard_map/while/body/eval_jaxpr/add | solution.py:87
  234.2 8.8 %multiply_add_fusion.4 = f32[16,4,1,2880]{3,2,1,0:T(1,128)S(1)} fusion(f32[16,4,1,2944]{3,2,1,0:T(1,128)S(1)} %get-tuple-element.535, s32[]{:T(128)S(6)} %select_n.276, s32[]{:T(128)S(6)} %select_n.277, s32[]{:T(128)S(6)} %select_n.278, s32[]{:T(128)S(6)} %select_n.279, s32[]{:T(128)S(6)} %select_n.280, f32[16,4,1,2880]{3,2,1,0:T(1,128)S(1)} %get-tuple-element.513, ...), kind=kLoop, calls=%fused_computation.4.clone.1 | loop fusion | flops 2027520 | bytes 5161301 | tf_op jit(solution)/shard_map/while/body/eval_jaxpr/add | solution.py:87
  243.0 8.8 %multiply_add_fusion.4 = f32[16,4,1,2880]{3,2,1,0:T(1,128)S(1)} fusion(f32[16,4,1,2944]{3,2,1,0:T(1,128)S(1)} %get-tuple-element.535, s32[]{:T(128)S(6)} %select_n.276, s32[]{:T(128)S(6)} %select_n.277, s32[]{:T(128)S(6)} %select_n.278, s32[]{:T(128)S(6)} %select_n.279, s32[]{:T(128)S(6)} %select_n.280, f32[16,4,1,2880]{3,2,1,0:T(1,128)S(1)} %get-tuple-element.513, ...), kind=kLoop, calls=%fused_computation.4.clone.1 | loop fusion | flops 2027520 | bytes 5161301 | tf_op jit(solution)/shard_map/while/body/eval_jaxpr/add | solution.py:87
  264.3 115.6 %while.33 = (s32[]{:T(128)}, f32[16,4,1,2880]{3,2,1,0:T(1,128)S(1)}, f32[16,65]{0,1:T(8,128)S(1)}, f32[16,4,1,2944]{3,2,1,0:T(1,128)S(1)}, s32[]{:T(128)}, /*ind...) while((s32[]{:T(128)}, ...), condition=%wide.region_3.4_spmd.clone, body=%wide.region_2.3_spmd.clone.sunk | while | flops 2027553 | bytes 5162514 | solution.py:96
  382.4 39.4 %all_to_all.70 = f32[64,4,1,2880]{3,1,2,0:T(4,128)S(1)} all-to-all(f32[64,4,1,2880]{3,1,2,0:T(4,128)S(1)} %maximum_bitcast_fusion), channel_id=1, replica_groups=mesh['lon'=8,'lat'=16] {'lat'}, dimensions={0} | all-to-all | bytes 5898240 | tf_op jit(solution)/shard_map/all_to_all | solution.py:144
  421.9 15.9 %copy.86 = f32[4,4,16,2880]{2,1,0,3:T(4,128)} copy(f32[4,4,16,2880]{3,1,0,2:T(4,128)S(1)} %bitcast.106) | data formatting | bytes 5898240 | tf_op jit(solution)/shard_map/all_to_all | solution.py:144
  437.8 19.6 %reshape.143 = f32[8,1,92160]{2,1,0:T(1,128)S(1)} reshape(f32[2880,4,4,16]{3,2,1,0:T(4,128)} %bitcast.102) | data formatting | bytes 5898240
  457.4 43.3 %all_to_all.71 = f32[8,1,92160]{2,1,0:T(1,128)} all-to-all(f32[8,1,92160]{2,1,0:T(1,128)S(1)} %reshape.143), channel_id=1, replica_groups=mesh['lon'=8,'lat'=16] {'lon'}, dimensions={0} | all-to-all | bytes 5898240 | tf_op jit(solution)/shard_map/all_to_all | solution.py:145
  501.2 9.7 %reduce = f32[8,92160]{1,0:T(8,128)S(1)} reduce(f32[8,1,92160]{2,1,0:T(1,128)} %all_to_all.71, f32[]{:T(128)} %broadcast.173), dimensions={1}, to_apply=%all_to_all.61.reduce_sub_computation | reduce | bytes 5898244 | tf_op jit(solution)/shard_map/all_to_all | solution.py:145
  510.9 25.0 %reshape.144 = f32[2880,4,4,16]{3,2,1,0:T(4,128)} reshape(f32[8,92160]{1,0:T(8,128)S(1)} %reduce) | data formatting | bytes 5898240
  535.8 17.1 %copy.90 = f32[4,4,16,8,360]{4,2,1,0,3:T(8,128)} copy(f32[4,4,16,8,360]{2,1,0,4,3:T(4,128)} %bitcast.103) | data formatting | bytes 5898240 | tf_op jit(solution)/shard_map/all_to_all | solution.py:145
  (107 shorter events, 177.2 us)
Async XLA Ops:
  0.0 93.1 %copy-start = (f32[256]{0:T(256)S(1)}, f32[256]{0:T(256)}, u32[]{:S(2)}) copy-start(f32[256]{0:T(256)} %param.9) | copy-start | bytes 3076
  3.2 11.2 %copy-start.2 = (f32[32,4,16,360]{3,2,1,0:T(8,128)S(1)}, f32[32,4,16,360]{3,2,1,0:T(8,128)}, u32[]{:S(2)}) copy-start(f32[32,4,16,360]{3,2,1,0:T(8,128)} %param.7) | copy-start | bytes 8847364
  5.2 7.9 %collective-permute-start.1 = (f32[32,4,16,1]{0,2,3,1:T(8,128)S(1)}, f32[32,4,16,1]{0,2,3,1:T(8,128)S(1)}, u32[]{:S(2)}, u32[]{:S(2)}) collective-permute-start(f32[32,4,16,1]{0,2,3,1:T(8,128)S(1)} %copy.92), channel_id=1, source_target_pairs={{16,0},{32,16},{48,32},{64,48},{80,64},{96,80},{112,96},{0,112},{1... | collective-permute-start | bytes 24584 | tf_op jit(solution)/shard_map/ppermute | solution.py:27
  8.4 3.2 collective-permute-start
  14.5 9.6 %copy-start.3 = (f32[32,4,16,1]{3,2,0,1:T(8,128)S(1)}, f32[32,4,16,1]{3,2,0,1:T(8,128)}, u32[]{:S(2)}) copy-start(f32[32,4,16,1]{3,2,0,1:T(8,128)} %copy.73) | copy-start | bytes 24580
  14.5 9.6 %copy-start.4 = (f32[32,4,16,1]{3,2,0,1:T(8,128)S(1)}, f32[32,4,16,1]{3,2,0,1:T(8,128)}, u32[]{:S(2)}) copy-start(f32[32,4,16,1]{3,2,0,1:T(8,128)} %copy.75) | copy-start | bytes 24580
  15.6 4.7 collective-permute-start.2
  18.7 5.4 collective-permute-start.3
  83.1 9.7 %copy-start.7 = (s32[256]{0:T(256)S(1)}, s32[256]{0:T(256)}, u32[]{:S(2)}) copy-start(s32[256]{0:T(256)} %param.8) | copy-start | bytes 3076
  83.1 53.6 %all-to-all-start.1 = ((f32[4,4,16,2880]{3,1,0,2:T(4,128)}), f32[4,4,16,2880]{3,1,0,2:T(4,128)}, u32[]{:S(2)}, u32[]{:S(2)}) async-start(f32[4,4,16,2880]{3,1,0,2:T(4,128)} %copy.80), calls=%async_computation.1 | async-start | bytes 6029312 | tf_op jit(solution)/shard_map/all_to_all | solution.py:137
  140.8 0.9 copy-start.5
  379.9 1.9 copy-start.6
  535.8 17.1 %copy-start.1 = (f32[256]{0:T(256)S(1)}, f32[256]{0:T(256)}, u32[]{:S(2)}) copy-start(f32[256]{0:T(256)} %param.9) | copy-start | bytes 3076
where the time goes:
time: 562 us; the launch traced here: 553 us
  other arithmetic  247 us (44%)
  blocking collectives  128 us (23%)
  local copies, waits for them, and re-layouts  109 us (19%)
  waiting for transfers between devices  48.5 us (9%)
  starting transfers between devices  16.8 us (3%)
    add x26, other arithmetic, add_one(): total + weight[:, None, None, None] * lax.dynamic_slice_in_dim(extended,...  229 us
    unnamed x22, local copies, waits for them, and re-layouts  52.8 us
    all_to_all x1, blocking collectives, shards(): lax.all_to_all(stepped, 'lon', split_axis=0, concat_axis=3, tiled=True)  45.6 us
    all_to_all x1, blocking collectives, shards(): lax.all_to_all(damped, 'lon', split_axis=3, concat_axis=0, tiled=True)  43.3 us
    all_to_all x1, waiting for transfers between devices, shards(): lax.all_to_all(gathered, 'lat', split_axis=2, concat_axis=0, tiled=True)  42.7 us
    all_to_all x1, blocking collectives, shards(): lax.all_to_all(spread, 'lat', split_axis=0, concat_axis=2, tiled=True)  39.4 us
    all_to_all x2, local copies, waits for them, and re-layouts, shards(): lax.all_to_all(damped, 'lon', split_axis=3, concat_axis=0, tiled=True)  17.6 us
    all_to_all x1, local copies, waits for them, and re-layouts, shards(): lax.all_to_all(spread, 'lat', split_axis=0, concat_axis=2, tiled=True)  15.9 us
  transfers between devices with their start and end apart: 5, of which 4 were waited for; matrix products, arithmetic and copies ran while one was open for 1% of the time, Pallas kernels for 0%

commit v1 on v0

v1 whole, which is shorter than its diff:
```python
import functools
import math

import jax
import jax.numpy as jnp
import numpy as np
from jax import lax
from jax.experimental import pallas as pl
from jax.experimental.pallas import tpu as pltpu
from jax.sharding import PartitionSpec as P

MAXB = 32
KX = 0.004
KY = 0.1
FC = 0.2

NLON_DEV = 8
NLAT_DEV = 16
ROWS = 32
NF = 4
LEV = 16
COLS = 360
LAST = COLS - 256
CHUNK = 4
NCHUNK = ROWS // CHUNK
MESH = pl.DeviceIdType.MESH
F32 = jnp.float32
BF16 = jnp.bfloat16


def row_table():
    total = ROWS * NLAT_DEV
    rows = np.arange(-1, total + 1, dtype=np.float32)
    angle = np.float32(math.pi) * ((rows + np.float32(0.5)) / np.float32(total) - np.float32(0.5))
    cos = np.cos(angle.astype(np.float64)).astype(np.float32)
    sin = np.sin(angle.astype(np.float64)).astype(np.float32)
    inv = np.float32(1.0) / cos
    table = np.zeros((NLAT_DEV, 8, 128), np.float32)
    for lat in range(NLAT_DEV):
        pad = slice(lat * ROWS, lat * ROWS + ROWS + 2)
        mid = slice(lat * ROWS + 1, lat * ROWS + ROWS + 1)
        table[lat, 0, : ROWS + 2] = cos[pad]
        table[lat, 1, :ROWS] = np.float32(KX) * inv[mid]
        table[lat, 2, :ROWS] = np.float32(KY) * inv[mid]
        table[lat, 3, :ROWS] = np.float32(FC) * sin[mid]
    return table


def kernel(
    state, band_hbm, damping_hbm, table_hbm, out,
    buf, to_east, to_west, from_west, from_east, x_east, x_west, xf_west, xf_east,
    edge, near, far, band, damping, table,
    load_sem, small_sem, send_sem, recv_sem, row_send, row_recv, x_send, x_recv, corner_send, corner_recv, ready,
):
    lon, lat = lax.axis_index("lon"), lax.axis_index("lat")
    east, west = lax.rem(lon + 1, NLON_DEV), lax.rem(lon + NLON_DEV - 1, NLON_DEV)
    north, south = lax.rem(lat + 1, NLAT_DEV), lax.rem(lat + NLAT_DEV - 1, NLAT_DEV)
    has_north, has_south = lat < NLAT_DEV - 1, lat > 0

    def at(a, b):
        return {"lon": a, "lat": b}

    def load(c):
        rows = pl.ds(c * CHUNK, CHUNK)
        return pltpu.make_async_copy(
            state.at[rows], buf.at[pl.ds(c * CHUNK + 1, CHUNK)], load_sem.at[c]
        )

    smalls = [
        pltpu.make_async_copy(band_hbm, band, small_sem.at[0]),
        pltpu.make_async_copy(damping_hbm, damping, small_sem.at[1]),
        pltpu.make_async_copy(table_hbm.at[lat], table, small_sem.at[2]),
    ]
    for c in range(NCHUNK):
        load(c).start()
    for copy in smalls:
        copy.start()

    barrier = pltpu.get_barrier_semaphore()
    for neighbour in (east, west):
        pl.semaphore_signal(barrier, 1, device_id=at(neighbour, lat), device_id_type=MESH)

    @pl.when(has_north)
    def _():
        pl.semaphore_signal(barrier, 1, device_id=at(lon, north), device_id_type=MESH)

    k = lax.broadcasted_iota(jnp.int32, (256, 128), 0)
    n = lax.broadcasted_iota(jnp.int32, (256, 128), 1)
    place = jnp.where(k < 192, k, k - 256)
    near[...] = jnp.minimum(jnp.abs(place - n), 255).astype(F32).astype(BF16)
    k = lax.broadcasted_iota(jnp.int32, (128, 256), 0)
    n = lax.broadcasted_iota(jnp.int32, (128, 256), 1)
    place = jnp.where(k >= 96, k - 128, jnp.where(k == 0, 0, jnp.where((k >= 31) & (k < 64), k + 328, 10000)))
    column = jnp.where(n < 128, n, n + 128)
    far[...] = jnp.minimum(jnp.abs(place - column), 255).astype(F32).astype(BF16)

    @pl.when(~has_south)
    def _():
        buf[0, 1:4] = jnp.zeros((3, LEV, COLS), F32)

    @pl.when(~has_north)
    def _():
        buf[ROWS + 1, 1:4] = jnp.zeros((3, LEV, COLS), F32)

    pl.semaphore_wait(barrier, 2 + jnp.where(has_south, 1, 0))

    def row_copy(i, target):
        source = state.at[ROWS - 1 if i == 0 else 0, pl.ds(1, 3)]
        goal = buf.at[0 if i == 0 else ROWS + 1, pl.ds(1, 3)]
        return pltpu.make_async_remote_copy(
            source, goal, row_send.at[i], row_recv.at[i], device_id=at(lon, target), device_id_type=MESH
        )

    @pl.when(has_south)
    def _():
        row_copy(1, south).start()
        pl.semaphore_signal(ready, 1, device_id=at(lon, south), device_id_type=MESH)

    lane = lax.broadcasted_iota(jnp.int32, (LEV, 128), 1)

    def tile(row, field, t):
        if t < 2:
            return buf[row, field, :, t * 128 : (t + 1) * 128]
        return jnp.concatenate([buf[row, field, :, 256:COLS], jnp.zeros((LEV, 128 - LAST), F32)], axis=1)

    def roll(a, shift):
        return pltpu.roll(a, shift, 1)

    def fixed(a, shift):
        return a if shift % 128 == 0 else pltpu.roll(a, shift % 128, 1)

    def pack(row, fields=range(NF)):
        for_east = jnp.zeros((LEV, 128), F32)
        for_west = jnp.zeros((LEV, 128), F32)
        for f in fields:
            here = (lane >= 32 * f) & (lane < 32 * f + 32)
            for_east = jnp.where(here, fixed(tile(row, f, 2), 32 * f - (LAST - 32)), for_east)
            for_west = jnp.where(here, fixed(tile(row, f, 0), 32 * f), for_west)
        return for_east, for_west

    def chunk_copy(c, i):
        source, goal, target = ((to_east, from_west, east), (to_west, from_east, west))[i]
        rows = pl.ds(c * CHUNK, CHUNK)
        return pltpu.make_async_remote_copy(
            source.at[rows], goal.at[rows], send_sem.at[i, c], recv_sem.at[i, c],
            device_id=at(target, lat), device_id_type=MESH,
        )

    def corner_copy(i, side):
        source, goal, target = ((to_east, from_west, east), (to_west, from_east, west))[side]
        return pltpu.make_async_remote_copy(
            source.at[ROWS + i], goal.at[ROWS + i], corner_send.at[side, i], corner_recv.at[side, i],
            device_id=at(target, lat), device_id_type=MESH,
        )

    def x_copy(side):
        source, goal, target = ((x_east, xf_west, east), (x_west, xf_east, west))[side]
        return pltpu.make_async_remote_copy(
            source, goal, x_send.at[side], x_recv.at[side], device_id=at(target, lat), device_id_type=MESH
        )

    def pack_chunk(c, carry):
        xe, xw = carry
        load(c).wait()
        for i in range(CHUNK):
            r = c * CHUNK + i
            to_east[r], to_west[r] = pack(r + 1)
            for slot, f in enumerate((0, 2, 3)):
                goal = 32 * slot + r
                here = lane == goal
                xe = jnp.where(here, roll(tile(r + 1, f, 2), lax.rem(goal + 256 - (LAST - 33), 128)), xe)
                xw = jnp.where(here, roll(tile(r + 1, f, 0), lax.rem(goal + 256 - 32, 128)), xw)
        chunk_copy(c, 0).start()
        chunk_copy(c, 1).start()
        return xe, xw

    xe, xw = lax.fori_loop(0, NCHUNK, pack_chunk, (jnp.zeros((LEV, 128), F32),) * 2)
    x_east[...] = xe
    x_west[...] = xw
    x_copy(0).start()
    x_copy(1).start()
    for copy in smalls:
        copy.wait()

    polar = (lat < NLAT_DEV // 4) | (lat >= NLAT_DEV - NLAT_DEV // 4)
    first = jnp.where(lat < NLAT_DEV // 4, lat * ROWS, jnp.where(polar, lat * ROWS - 256, 0))

    def coefficients(r):
        width = jnp.full((LEV, 128), band[first + r], jnp.int32).astype(F32) + 1.0
        strength = jnp.full((LEV, 128), jnp.where(polar, damping[first + r], 0.0), F32)
        return width, 1.0 - strength, strength / (width * width)

    def weights(distances, width):
        top = width.astype(BF16)
        rows, columns = distances.shape
        top = jnp.concatenate([top] * (rows // LEV), axis=0)
        top = jnp.concatenate([top] * (columns // 128), axis=1)
        return jnp.maximum(top - distances[...], jnp.zeros((), BF16))

    def step(r, mid, up, down, diff):
        kx, ky, fs = table[1, r], table[2, r], table[3, r]
        u, v, h, q = (mid(f) for f in range(NF))
        vn, hn, qn = (up(f) for f in (1, 2, 3))
        vs, hs, qs = (down(f) for f in (1, 2, 3))
        flux = vn * hn * table[0, r + 2] - vs * hs * table[0, r]
        d_flux, d_h, d_q = diff
        h_new = h - kx * d_flux - ky * flux
        u_new = u - kx * d_h + fs * v
        v_new = v - KY * (hn - hs) - fs * u
        q_new = q - kx * u * d_q - KY * v * (qn - qs)
        return u_new, v_new, h_new, q_new

    def halves(a):
        high = a.astype(BF16)
        return high, (a - high.astype(F32)).astype(BF16)

    def product(left, right):
        return jnp.dot(left, right, preferred_element_type=F32)

    def early(r):
        row = r + 1
        width, keep, gain = coefficients(r)
        mids = [[tile(row, f, t) for t in range(3)] for f in range(NF)]

        def difference(tiles):
            lo = [roll(a, 127) for a in tiles]
            hi = [roll(a, 1) for a in tiles]
            result = []
            for t in range(3):
                e = lo[t] if t == 2 else jnp.where(lane == 127, lo[t + 1], lo[t])
                w = hi[t] if t == 0 else jnp.where(lane == 0, hi[t - 1], hi[t])
                result.append(e - w)
            return result

        d_flux = difference([mids[0][t] * mids[2][t] for t in range(3)])
        d_h = difference(mids[2])
        d_q = difference(mids[3])
        stepped = []
        for t in range(3):
            values = step(
                r, lambda f: mids[f][t], lambda f: tile(row + 1, f, t), lambda f: tile(row - 1, f, t),
                (d_flux[t], d_h[t], d_q[t]),
            )
            if t == 0:
                values = [jnp.where(lane == 0, 0.0, a) for a in values]
            if t == 2:
                values = [jnp.where(lane >= LAST - 1, 0.0, a) for a in values]
            stepped.append(values)
        right = weights(near, width)
        parts = [[halves(a) for a in values] for values in stepped]
        zero = jnp.zeros((LEV, 128), BF16)

        def left(half):
            blocks = []
            for t in range(3):
                for f in range(NF):
                    after = parts[t + 1][f][half] if t < 2 else zero
                    before = parts[t - 1][f][half] if t > 0 else zero
                    side = jnp.where(lane < 64, after, before)
                    blocks.append(jnp.concatenate([parts[t][f][half], side], axis=1))
            return jnp.concatenate(blocks, axis=0)

        smooth = product(left(0), right) + product(left(1), right)
        for t in range(3):
            for f in range(NF):
                place = (t * NF + f) * LEV
                value = keep * stepped[t][f] + gain * smooth[place : place + LEV]
                if t < 2:
                    out[r, f, :, t * 128 : (t + 1) * 128] = value
                else:
                    out[r, f, :, 256:COLS] = value[:, :LAST]

    def unpack(slot, row, fields=range(NF), extra=None):
        got_west, got_east = from_west[slot], from_east[slot]
        for f in fields:
            own = jnp.where(lane < 2, tile(row, f, 0), fixed(tile(row, f, 2), 31 - (LAST - 1)))
            halo = jnp.where(lane >= 96, fixed(got_west, 96 - 32 * f), fixed(got_east, 32 - 32 * f))
            value = jnp.where(lane < 32, own, halo)
            if extra is not None and f != 1:
                goal = 32 * (0, None, 1, 2)[f] + extra
                value = jnp.where(lane == 95, roll(xf_west[...], lax.rem(95 + 256 - goal, 128)), value)
                value = jnp.where(lane == 64, roll(xf_east[...], lax.rem(64 + 256 - goal, 128)), value)
            edge[row, f] = value

    def late(r):
        row = r + 1
        width, keep, gain = coefficients(r)

        def difference(a):
            return roll(a, 127) - roll(a, 1)

        mids = [edge[row, f] for f in range(NF)]
        stepped = step(
            r, lambda f: mids[f], lambda f: edge[row + 1, f], lambda f: edge[row - 1, f],
            (difference(mids[0] * mids[2]), difference(mids[2]), difference(mids[3])),
        )
        right = weights(far, width)
        parts = [halves(a) for a in stepped]
        smooth = product(jnp.concatenate([p[0] for p in parts], axis=0), right) + product(
            jnp.concatenate([p[1] for p in parts], axis=0), right
        )
        for f in range(NF):
            more = gain * smooth[f * LEV : (f + 1) * LEV, :128] + jnp.where(lane == 0, keep * stepped[f], 0.0)
            out[r, f, :, 0:128] = out[r, f, :, 0:128] + more
            last = roll(stepped[f], LAST - 1 - 31)
            more = gain * smooth[f * LEV : (f + 1) * LEV, 128:] + jnp.where(lane == LAST - 1, keep * last, 0.0)
            out[r, f, :, 256:COLS] = out[r, f, :, 256:COLS] + more[:, :LAST]

    def rows(begin, end, body):
        def run(r, carry):
            body(r)
            return carry

        lax.fori_loop(begin, end, run, 0)

    rows(1, 8, early)

    @pl.when(has_north)
    def _():
        pl.semaphore_wait(ready, 1)
        row_copy(0, north).start()

    rows(8, 22, early)

    @pl.when(has_north)
    def _():
        row_copy(1, north).wait_recv()

    @pl.when(has_south)
    def _():
        row_copy(0, south).wait_recv()

    for i, row in enumerate((0, ROWS + 1)):
        to_east[ROWS + i], to_west[ROWS + i] = pack(row, (1, 2, 3))
        for side in range(2):
            corner_copy(i, side).start()
    rows(22, ROWS, early)
    early(0)

    for side in range(2):
        x_copy(side).wait()

    def late_chunk(c, carry):
        for side in range(2):
            chunk_copy(c, side).wait()
        for i in range(CHUNK):
            unpack(c * CHUNK + i, c * CHUNK + i + 1, extra=c * CHUNK + i)
        rows(jnp.maximum(c * CHUNK - 1, 1), c * CHUNK + CHUNK - 1, late)
        return carry

    lax.fori_loop(0, NCHUNK, late_chunk, 0)
    for i, row in enumerate((0, ROWS + 1)):
        for side in range(2):
            corner_copy(i, side).wait()
        unpack(ROWS + i, row, (1, 2, 3))
    late(0)
    late(ROWS - 1)

    @pl.when(has_north)
    def _():
        row_copy(0, north).wait_send()

    @pl.when(has_south)
    def _():
        row_copy(1, south).wait_send()


def shards(state, band, damping):
    hbm = pl.BlockSpec(memory_space=pl.ANY)
    packed = pltpu.VMEM((ROWS + 2, LEV, 128), F32)
    extra = pltpu.VMEM((LEV, 128), F32)
    dma = pltpu.SemaphoreType.DMA
    return pl.pallas_call(
        kernel,
        out_shape=pltpu.VMEM(state.shape, F32),
        in_specs=[hbm] * 4,
        out_specs=pl.BlockSpec(memory_space=pltpu.VMEM),
        scratch_shapes=[
            pltpu.VMEM((ROWS + 2, NF, LEV, COLS), F32),
            packed, packed, packed, packed,
            extra, extra, extra, extra,
            pltpu.VMEM((ROWS + 2, NF, LEV, 128), F32),
            pltpu.VMEM((256, 128), BF16),
            pltpu.VMEM((128, 256), BF16),
            pltpu.SMEM((256,), jnp.int32),
            pltpu.SMEM((256,), F32),
            pltpu.SMEM((8, 128), F32),
            dma((NCHUNK,)), dma((3,)),
            dma((2, NCHUNK)), dma((2, NCHUNK)),
            dma((2,)), dma((2,)),
            dma((2,)), dma((2,)),
            dma((2, 2)), dma((2, 2)),
            pltpu.SemaphoreType.REGULAR,
        ],
        compiler_params=pltpu.CompilerParams(
            collective_id=0, has_side_effects=True, vmem_limit_bytes=32 * 1024 * 1024
        ),
    )(state, band, damping, jnp.asarray(row_table()))


def solution(mesh):
    in_specs = (P("lat", None, None, "lon"), P(), P())
    out_specs = P("lat", None, None, "lon")
    return jax.shard_map(shards, mesh=mesh, in_specs=in_specs, out_specs=out_specs, check_vma=False)
```

time: 562 us -> 30.7 us (0.05)
  the two profiles are of different devices: /device:TPU:1 before, /device:TPU:32 now
where the time goes in v1:
time: 30.7 us; the launch traced here: 30.2 us
  Pallas kernels  24.4 us (79%)
  local copies, waits for them, and re-layouts  5.75 us (19%)
    pallas_call x1, Pallas kernels, shards(): pl.pallas_call(kernel, out_shape=pltpu.VMEM(state.shape, F32), in_specs=[...  24.4 us
    unnamed x9, local copies, waits for them, and re-layouts  5.75 us

profile of v1, /device:TPU:32, one launch (start us, length us, event | category | flops | bytes accessed | tf_op | source)
XLA Modules:
  0.0 30.2 jit_solution(4063565761473177738)
XLA Ops:
  0.0 0.0 copy-start
  0.0 1.9 %copy-done = f32[32,4,16,360]{3,2,1,0:T(8,128)S(1)} copy-done((f32[32,4,16,360]{3,2,1,0:T(8,128)S(1)}, f32[32,4,16,360]{3,2,1,0:T(8,128)}, u32[]{:S(2)}) %copy-start) | copy-done | bytes 2949144
  1.9 0.0 copy-start.1
  1.9 0.8 %copy-done.1 = f32[16,8,128]{2,1,0:T(8,128)S(1)} copy-done((f32[16,8,128]{2,1,0:T(8,128)S(1)}, f32[16,8,128]{2,1,0:T(8,128)}, u32[]{:S(2)}) %copy-start.1) | copy-done | bytes 65560
  2.7 0.0 copy-start.2
  2.7 0.7 %copy-done.2 = s32[256]{0:T(256)S(1)} copy-done((s32[256]{0:T(256)S(1)}, s32[256]{0:T(256)}, u32[]{:S(2)}) %copy-start.2) | copy-done | bytes 1048
  3.4 0.0 copy-start.3
  3.4 0.7 %copy-done.3 = f32[256]{0:T(256)S(1)} copy-done((f32[256]{0:T(256)S(1)}, f32[256]{0:T(256)}, u32[]{:S(2)}) %copy-start.3) | copy-done | bytes 1048
  4.1 24.4 %shard_map.46 = f32[32,4,16,360]{3,2,1,0:T(8,128)S(1)} custom-call(f32[32,4,16,360]{3,2,1,0:T(8,128)S(1)} %copy-done, s32[256]{0:T(256)S(1)} %copy-done.2, f32[256]{0:T(256)S(1)} %copy-done.3, f32[16,8,128]{2,1,0:T(8,128)S(1)} %copy-done.1), custom_call_target="tpu_custom_call" | custom-call | tf_op jit(solution)/shard_map/pallas_call | solution.py:373
  28.5 1.7 %copy.6 = f32[32,4,16,360]{3,2,1,0:T(8,128)} copy(f32[32,4,16,360]{3,2,1,0:T(8,128)S(1)} %shard_map.46) | data formatting | bytes 5898240
Async XLA Ops:
  0.0 1.9 %copy-start = (f32[32,4,16,360]{3,2,1,0:T(8,128)S(1)}, f32[32,4,16,360]{3,2,1,0:T(8,128)}, u32[]{:S(2)}) copy-start(f32[32,4,16,360]{3,2,1,0:T(8,128)} %state.1) | copy-start | bytes 8847364
  1.9 0.8 %copy-start.1 = (f32[16,8,128]{2,1,0:T(8,128)S(1)}, f32[16,8,128]{2,1,0:T(8,128)}, u32[]{:S(2)}) copy-start(f32[16,8,128]{2,1,0:T(8,128)} %constant.2.clone.table_hbm) | copy-start | bytes 196612
  2.7 0.7 %copy-start.2 = (s32[256]{0:T(256)S(1)}, s32[256]{0:T(256)}, u32[]{:S(2)}) copy-start(s32[256]{0:T(256)} %band_hbm.1) | copy-start | bytes 3076
  3.4 0.7 %copy-start.3 = (f32[256]{0:T(256)S(1)}, f32[256]{0:T(256)}, u32[]{:S(2)}) copy-start(f32[256]{0:T(256)} %damping_hbm.1) | copy-start | bytes 3076

commit v2 on v1

--- a/solution.py
+++ b/solution.py
@@ -16,13 +16,15 @@
 
 NLON_DEV = 8
 NLAT_DEV = 16
+NX = 4
 ROWS = 32
 NF = 4
 LEV = 16
 COLS = 360
 LAST = COLS - 256
-CHUNK = 4
+CHUNK = 2
 NCHUNK = ROWS // CHUNK
+GROUP = 8
 MESH = pl.DeviceIdType.MESH
 F32 = jnp.float32
 BF16 = jnp.bfloat16
@@ -48,7 +50,7 @@
 
 def kernel(
     state, band_hbm, damping_hbm, table_hbm, out,
-    buf, to_east, to_west, from_west, from_east, x_east, x_west, xf_west, xf_east,
+    buf, to_east, to_west, from_west, from_east, x_east, x_west, xf_west, xf_east, x_both,
     edge, near, far, band, damping, table,
     load_sem, small_sem, send_sem, recv_sem, row_send, row_recv, x_send, x_recv, corner_send, corner_recv, ready,
 ):
@@ -56,6 +58,9 @@
     east, west = lax.rem(lon + 1, NLON_DEV), lax.rem(lon + NLON_DEV - 1, NLON_DEV)
     north, south = lax.rem(lat + 1, NLAT_DEV), lax.rem(lat + NLAT_DEV - 1, NLAT_DEV)
     has_north, has_south = lat < NLAT_DEV - 1, lat > 0
+    x = lax.rem(lat, NX)
+    first_north, first_south = x < NX - 1, (x == 0) & has_south
+    second_north, second_south = (x == NX - 1) & has_north, x > 0
 
     def at(a, b):
         return {"lon": a, "lat": b}
@@ -80,9 +85,13 @@
     for neighbour in (east, west):
         pl.semaphore_signal(barrier, 1, device_id=at(neighbour, lat), device_id_type=MESH)
 
-    @pl.when(has_north)
+    @pl.when(first_north)
     def _():
         pl.semaphore_signal(barrier, 1, device_id=at(lon, north), device_id_type=MESH)
+
+    @pl.when(first_south)
+    def _():
+        pl.semaphore_signal(barrier, 1, device_id=at(lon, south), device_id_type=MESH)
 
     k = lax.broadcasted_iota(jnp.int32, (256, 128), 0)
     n = lax.broadcasted_iota(jnp.int32, (256, 128), 1)
@@ -90,7 +99,7 @@
     near[...] = jnp.minimum(jnp.abs(place - n), 255).astype(F32).astype(BF16)
     k = lax.broadcasted_iota(jnp.int32, (128, 256), 0)
     n = lax.broadcasted_iota(jnp.int32, (128, 256), 1)
-    place = jnp.where(k >= 96, k - 128, jnp.where(k == 0, 0, jnp.where((k >= 31) & (k < 64), k + 328, 10000)))
+    place = jnp.where(k >= 96, k - 128, jnp.where(k == 0, 0, jnp.where((k >= 30) & (k < 63), k + 329, 10000)))
     column = jnp.where(n < 128, n, n + 128)
     far[...] = jnp.minimum(jnp.abs(place - column), 255).astype(F32).astype(BF16)
 
@@ -102,7 +111,7 @@
     def _():
         buf[ROWS + 1, 1:4] = jnp.zeros((3, LEV, COLS), F32)
 
-    pl.semaphore_wait(barrier, 2 + jnp.where(has_south, 1, 0))
+    pl.semaphore_wait(barrier, 2 + jnp.where(second_south, 1, 0) + jnp.where(second_north, 1, 0))
 
     def row_copy(i, target):
         source = state.at[ROWS - 1 if i == 0 else 0, pl.ds(1, 3)]
@@ -111,10 +120,15 @@
             source, goal, row_send.at[i], row_recv.at[i], device_id=at(lon, target), device_id_type=MESH
         )
 
-    @pl.when(has_south)
+    @pl.when(second_south)
     def _():
         row_copy(1, south).start()
-        pl.semaphore_signal(ready, 1, device_id=at(lon, south), device_id_type=MESH)
+        pl.semaphore_signal(ready.at[0], 1, device_id=at(lon, south), device_id_type=MESH)
+
+    @pl.when(second_north)
+    def _():
+        row_copy(0, north).start()
+        pl.semaphore_signal(ready.at[1], 1, device_id=at(lon, north), device_id_type=MESH)
 
     lane = lax.broadcasted_iota(jnp.int32, (LEV, 128), 1)
 
@@ -260,7 +274,8 @@
                     blocks.append(jnp.concatenate([parts[t][f][half], side], axis=1))
             return jnp.concatenate(blocks, axis=0)
 
-        smooth = product(left(0), right) + product(left(1), right)
+        both = product(jnp.concatenate([left(0), left(1)], axis=0), right)
+        smooth = both[: both.shape[0] // 2] + both[both.shape[0] // 2 :]
         for t in range(3):
             for f in range(NF):
                 place = (t * NF + f) * LEV
@@ -273,13 +288,12 @@
     def unpack(slot, row, fields=range(NF), extra=None):
         got_west, got_east = from_west[slot], from_east[slot]
         for f in fields:
-            own = jnp.where(lane < 2, tile(row, f, 0), fixed(tile(row, f, 2), 31 - (LAST - 1)))
-            halo = jnp.where(lane >= 96, fixed(got_west, 96 - 32 * f), fixed(got_east, 32 - 32 * f))
-            value = jnp.where(lane < 32, own, halo)
+            own = jnp.where(lane < 2, tile(row, f, 0), fixed(tile(row, f, 2), 30 - (LAST - 1)))
+            halo = jnp.where(lane >= 96, fixed(got_west, 96 - 32 * f), fixed(got_east, 31 - 32 * f))
+            value = jnp.where(lane < 31, own, halo)
             if extra is not None and f != 1:
-                goal = 32 * (0, None, 1, 2)[f] + extra
-                value = jnp.where(lane == 95, roll(xf_west[...], lax.rem(95 + 256 - goal, 128)), value)
-                value = jnp.where(lane == 64, roll(xf_east[...], lax.rem(64 + 256 - goal, 128)), value)
+                outer = roll(x_both[(0, None, 1, 2)[f]], 63 - extra)
+                value = jnp.where((lane == 63) | (lane == 95), outer, value)
             edge[row, f] = value
 
     def late(r):
@@ -296,31 +310,34 @@
         )
         right = weights(far, width)
         parts = [halves(a) for a in stepped]
-        smooth = product(jnp.concatenate([p[0] for p in parts], axis=0), right) + product(
-            jnp.concatenate([p[1] for p in parts], axis=0), right
-        )
+        left = jnp.concatenate([jnp.concatenate(p, axis=1) for p in parts], axis=0)
+        smooth = product(left, jnp.concatenate([right, right], axis=0))
         for f in range(NF):
             more = gain * smooth[f * LEV : (f + 1) * LEV, :128] + jnp.where(lane == 0, keep * stepped[f], 0.0)
             out[r, f, :, 0:128] = out[r, f, :, 0:128] + more
-            last = roll(stepped[f], LAST - 1 - 31)
+            last = roll(stepped[f], LAST - 1 - 30)
             more = gain * smooth[f * LEV : (f + 1) * LEV, 128:] + jnp.where(lane == LAST - 1, keep * last, 0.0)
             out[r, f, :, 256:COLS] = out[r, f, :, 256:COLS] + more[:, :LAST]
 
-    def rows(begin, end, body):
-        def run(r, carry):
-            body(r)
-            return carry
-
-        lax.fori_loop(begin, end, run, 0)
-
-    rows(1, 8, early)
-
-    @pl.when(has_north)
-    def _():
-        pl.semaphore_wait(ready, 1)
+    for i in range(GROUP):
+        early(1 + i)
+
+    @pl.when(first_north)
+    def _():
+        pl.semaphore_wait(ready.at[0], 1)
         row_copy(0, north).start()
 
-    rows(8, 22, early)
+    @pl.when(first_south)
+    def _():
+        pl.semaphore_wait(ready.at[1], 1)
+        row_copy(1, south).start()
+
+    def early_group(g, carry):
+        for i in range(GROUP):
+            early(g * GROUP + 1 + i)
+        return carry
+
+    lax.fori_loop(1, 3, early_group, 0)
 
     @pl.when(has_north)
     def _():
@@ -334,27 +351,42 @@
         to_east[ROWS + i], to_west[ROWS + i] = pack(row, (1, 2, 3))
         for side in range(2):
             corner_copy(i, side).start()
-    rows(22, ROWS, early)
-    early(0)
+    for r in (*range(3 * GROUP + 1, ROWS), 0):
+        early(r)
 
     for side in range(2):
         x_copy(side).wait()
-
-    def late_chunk(c, carry):
+    for slot in range(3):
+        x_both[slot] = jnp.where(lane < 32, fixed(xf_east[...], -32 * slot), fixed(xf_west[...], 32 - 32 * slot))
+
+    def arrived(c):
         for side in range(2):
             chunk_copy(c, side).wait()
         for i in range(CHUNK):
             unpack(c * CHUNK + i, c * CHUNK + i + 1, extra=c * CHUNK + i)
-        rows(jnp.maximum(c * CHUNK - 1, 1), c * CHUNK + CHUNK - 1, late)
+
+    arrived(0)
+
+    def late_group(g, carry):
+        for i in range(GROUP // CHUNK):
+            for side in range(2):
+                chunk_copy(g * (GROUP // CHUNK) + 1 + i, side).wait()
+        for i in range(GROUP):
+            r = g * GROUP + CHUNK + i
+            unpack(r, r + 1, extra=r)
+        for i in range(GROUP):
+            late(g * GROUP + 1 + i)
         return carry
 
-    lax.fori_loop(0, NCHUNK, late_chunk, 0)
+    lax.fori_loop(0, 3, late_group, 0)
+    for c in range(3 * GROUP // CHUNK + 1, NCHUNK):
+        arrived(c)
     for i, row in enumerate((0, ROWS + 1)):
         for side in range(2):
             corner_copy(i, side).wait()
         unpack(ROWS + i, row, (1, 2, 3))
-    late(0)
-    late(ROWS - 1)
+    for r in (*range(3 * GROUP + 1, ROWS), 0):
+        late(r)
 
     @pl.when(has_north)
     def _():
@@ -366,7 +398,7 @@
 
 
 def shards(state, band, damping):
-    hbm = pl.BlockSpec(memory_space=pl.ANY)
+    hbm = pl.BlockSpec(memory_space=pltpu.HBM)
     packed = pltpu.VMEM((ROWS + 2, LEV, 128), F32)
     extra = pltpu.VMEM((LEV, 128), F32)
     dma = pltpu.SemaphoreType.DMA
@@ -379,6 +411,7 @@
             pltpu.VMEM((ROWS + 2, NF, LEV, COLS), F32),
             packed, packed, packed, packed,
             extra, extra, extra, extra,
+            pltpu.VMEM((3, LEV, 128), F32),
             pltpu.VMEM((ROWS + 2, NF, LEV, 128), F32),
             pltpu.VMEM((256, 128), BF16),
             pltpu.VMEM((128, 256), BF16),
@@ -390,10 +423,10 @@
             dma((2,)), dma((2,)),
             dma((2,)), dma((2,)),
             dma((2, 2)), dma((2, 2)),
-            pltpu.SemaphoreType.REGULAR,
+            pltpu.SemaphoreType.REGULAR((2,)),
         ],
         compiler_params=pltpu.CompilerParams(
-            collective_id=0, has_side_effects=True, vmem_limit_bytes=32 * 1024 * 1024
+            collective_id=0, has_side_effects=True, vmem_limit_bytes=60 * 1024 * 1024
         ),
     )(state, band, damping, jnp.asarray(row_table()))
 

time: 30.7 us -> 16.1 us (0.52)
  the two profiles are of different devices: /device:TPU:32 before, /device:TPU:38 now
where the time goes in v2:
time: 16.1 us; the launch traced here: 16 us
  Pallas kernels  14.3 us (89%)
  local copies, waits for them, and re-layouts  1.67 us (10%)
    pallas_call x1, Pallas kernels, shards(): pl.pallas_call(kernel, out_shape=pltpu.VMEM(state.shape, F32), in_specs=[...  14.3 us
    unnamed x1, local copies, waits for them, and re-layouts  1.67 us

profile of v2, /device:TPU:38, one launch (start us, length us, event | category | flops | bytes accessed | tf_op | source)
XLA Modules:
  0.0 16.0 jit_solution(13944079452434077625)
XLA Ops:
  0.0 14.3 %shard_map.46 = f32[32,4,16,360]{3,2,1,0:T(8,128)S(1)} custom-call(f32[32,4,16,360]{3,2,1,0:T(8,128)} %state.1, s32[256]{0:T(256)} %band_hbm.1, f32[256]{0:T(256)} %damping_hbm.1, f32[16,8,128]{2,1,0:T(8,128)} %constant.2.clone.table_hbm), custom_call_target="tpu_custom_call" | custom-call | tf_op jit(solution)/shard_map/pallas_call | solution.py:405
  14.3 1.7 %copy.6 = f32[32,4,16,360]{3,2,1,0:T(8,128)} copy(f32[32,4,16,360]{3,2,1,0:T(8,128)S(1)} %shard_map.46) | data formatting | bytes 5898240

commit v3 on v2

--- a/solution.py
+++ b/solution.py
@@ -22,7 +22,7 @@
 LEV = 16
 COLS = 360
 LAST = COLS - 256
-CHUNK = 2
+CHUNK = 4
 NCHUNK = ROWS // CHUNK
 GROUP = 8
 MESH = pl.DeviceIdType.MESH
@@ -52,15 +52,21 @@
     state, band_hbm, damping_hbm, table_hbm, out,
     buf, to_east, to_west, from_west, from_east, x_east, x_west, xf_west, xf_east, x_both,
     edge, near, far, band, damping, table,
-    load_sem, small_sem, send_sem, recv_sem, row_send, row_recv, x_send, x_recv, corner_send, corner_recv, ready,
+    load_sem, small_sem, send_sem, recv_sem, row_send, row_recv, x_send, x_recv, ready,
 ):
     lon, lat = lax.axis_index("lon"), lax.axis_index("lat")
     east, west = lax.rem(lon + 1, NLON_DEV), lax.rem(lon + NLON_DEV - 1, NLON_DEV)
     north, south = lax.rem(lat + 1, NLAT_DEV), lax.rem(lat + NLAT_DEV - 1, NLAT_DEV)
     has_north, has_south = lat < NLAT_DEV - 1, lat > 0
     x = lax.rem(lat, NX)
-    first_north, first_south = x < NX - 1, (x == 0) & has_south
-    second_north, second_south = (x == NX - 1) & has_north, x > 0
+    polar = (lat < NLAT_DEV // 4) | (lat >= NLAT_DEV - NLAT_DEV // 4)
+    crossing = ((x == NX - 1) & has_north) | ((x == 0) & has_south)
+    last_south, first_mid = lat == NLAT_DEV // 4 - 1, lat == NLAT_DEV // 4
+    first = ((x < NX - 1) | last_south, (x == 0) & has_south & ~first_mid, lon < NLON_DEV - 1, lon == 0)
+    second = ((x == NX - 1) & has_north & ~last_south, (x > 0) | first_mid, lon == NLON_DEV - 1, lon > 0)
+    others = ((lon, north), (lon, south), (east, lat), (west, lat))
+    NORTH, SOUTH, EAST, WEST = range(4)
+    OPPOSITE = (SOUTH, NORTH, WEST, EAST)
 
     def at(a, b):
         return {"lon": a, "lat": b}
@@ -82,16 +88,15 @@
         copy.start()
 
     barrier = pltpu.get_barrier_semaphore()
-    for neighbour in (east, west):
-        pl.semaphore_signal(barrier, 1, device_id=at(neighbour, lat), device_id_type=MESH)
-
-    @pl.when(first_north)
-    def _():
-        pl.semaphore_signal(barrier, 1, device_id=at(lon, north), device_id_type=MESH)
-
-    @pl.when(first_south)
-    def _():
-        pl.semaphore_signal(barrier, 1, device_id=at(lon, south), device_id_type=MESH)
+    for side in range(4):
+
+        @pl.when(first[side])
+        def _():
+            pl.semaphore_signal(barrier, 1, device_id=at(*others[side]), device_id_type=MESH)
+
+    @pl.when(lon == 1)
+    def _():
+        pl.semaphore_signal(barrier, 1, device_id=at(west, lat), device_id_type=MESH)
 
     k = lax.broadcasted_iota(jnp.int32, (256, 128), 0)
     n = lax.broadcasted_iota(jnp.int32, (256, 128), 1)
@@ -111,7 +116,12 @@
     def _():
         buf[ROWS + 1, 1:4] = jnp.zeros((3, LEV, COLS), F32)
 
-    pl.semaphore_wait(barrier, 2 + jnp.where(second_south, 1, 0) + jnp.where(second_north, 1, 0))
+    @pl.when(~polar)
+    def _():
+        from_west[...] = jnp.zeros(from_west.shape, F32)
+        from_east[...] = jnp.zeros(from_east.shape, F32)
+
+    pl.semaphore_wait(barrier, sum(jnp.where(flag, 1, 0) for flag in (*second, lon == 0)))
 
     def row_copy(i, target):
         source = state.at[ROWS - 1 if i == 0 else 0, pl.ds(1, 3)]
@@ -120,15 +130,19 @@
             source, goal, row_send.at[i], row_recv.at[i], device_id=at(lon, target), device_id_type=MESH
         )
 
-    @pl.when(second_south)
+    @pl.when(second[SOUTH])
     def _():
         row_copy(1, south).start()
-        pl.semaphore_signal(ready.at[0], 1, device_id=at(lon, south), device_id_type=MESH)
-
-    @pl.when(second_north)
+
+    @pl.when(second[NORTH])
     def _():
         row_copy(0, north).start()
-        pl.semaphore_signal(ready.at[1], 1, device_id=at(lon, north), device_id_type=MESH)
+
+    for side in range(4):
+
+        @pl.when(second[side])
+        def _():
+            pl.semaphore_signal(ready.at[OPPOSITE[side]], 1, device_id=at(*others[side]), device_id_type=MESH)
 
     lane = lax.broadcasted_iota(jnp.int32, (LEV, 128), 1)
 
@@ -160,10 +174,11 @@
             device_id=at(target, lat), device_id_type=MESH,
         )
 
-    def corner_copy(i, side):
-        source, goal, target = ((to_east, from_west, east), (to_west, from_east, west))[side]
+    def corner_copy(i):
+        source, goal, target = ((to_east, from_west, east), (to_west, from_east, west))[i]
+        rows = pl.ds(ROWS, 2)
         return pltpu.make_async_remote_copy(
-            source.at[ROWS + i], goal.at[ROWS + i], corner_send.at[side, i], corner_recv.at[side, i],
+            source.at[rows], goal.at[rows], send_sem.at[i, NCHUNK], recv_sem.at[i, NCHUNK],
             device_id=at(target, lat), device_id_type=MESH,
         )
 
@@ -182,26 +197,62 @@
             for slot, f in enumerate((0, 2, 3)):
                 goal = 32 * slot + r
                 here = lane == goal
-                xe = jnp.where(here, roll(tile(r + 1, f, 2), lax.rem(goal + 256 - (LAST - 33), 128)), xe)
-                xw = jnp.where(here, roll(tile(r + 1, f, 0), lax.rem(goal + 256 - 32, 128)), xw)
-        chunk_copy(c, 0).start()
-        chunk_copy(c, 1).start()
+                xe = jnp.where(here, roll(tile(r + 1, f, 2), lax.rem(goal + 256 - jnp.where(polar, LAST - 33, LAST - 1), 128)), xe)
+                xw = jnp.where(here, roll(tile(r + 1, f, 0), lax.rem(goal + 256 - jnp.where(polar, 32, 0), 128)), xw)
+
+        @pl.when(polar & second[EAST])
+        def _():
+            chunk_copy(c, 0).start()
+
+        @pl.when(polar & second[WEST])
+        def _():
+            chunk_copy(c, 1).start()
+
         return xe, xw
 
     xe, xw = lax.fori_loop(0, NCHUNK, pack_chunk, (jnp.zeros((LEV, 128), F32),) * 2)
     x_east[...] = xe
     x_west[...] = xw
-    x_copy(0).start()
-    x_copy(1).start()
+
+    def send_side(i):
+        pl.semaphore_wait(ready.at[(EAST, WEST)[i]], 1)
+
+        def send(c, carry):
+            chunk_copy(c, i).start()
+            return carry
+
+        lax.fori_loop(0, jnp.where(polar, NCHUNK, 0), send, 0)
+        x_copy(i).start()
+
+    @pl.when(second[EAST])
+    def _():
+        x_copy(0).start()
+
+    @pl.when(second[WEST])
+    def _():
+        x_copy(1).start()
+
+    @pl.when(first[EAST])
+    def _():
+        send_side(0)
+
+    @pl.when(first[NORTH] & ~last_south)
+    def _():
+        pl.semaphore_wait(ready.at[NORTH], 1)
+        row_copy(0, north).start()
+
+    @pl.when(first[WEST])
+    def _():
+        send_side(1)
+
     for copy in smalls:
         copy.wait()
 
-    polar = (lat < NLAT_DEV // 4) | (lat >= NLAT_DEV - NLAT_DEV // 4)
-    first = jnp.where(lat < NLAT_DEV // 4, lat * ROWS, jnp.where(polar, lat * ROWS - 256, 0))
+    origin = jnp.where(lat < NLAT_DEV // 4, lat * ROWS, jnp.where(polar, lat * ROWS - 256, 0))
 
     def coefficients(r):
-        width = jnp.full((LEV, 128), band[first + r], jnp.int32).astype(F32) + 1.0
-        strength = jnp.full((LEV, 128), jnp.where(polar, damping[first + r], 0.0), F32)
+        width = jnp.full((LEV, 128), band[origin + r], jnp.int32).astype(F32) + 1.0
+        strength = jnp.full((LEV, 128), jnp.where(polar, damping[origin + r], 0.0), F32)
         return width, 1.0 - strength, strength / (width * width)
 
     def weights(distances, width):
@@ -285,15 +336,18 @@
                 else:
                     out[r, f, :, 256:COLS] = value[:, :LAST]
 
-    def unpack(slot, row, fields=range(NF), extra=None):
+    outer_lanes = (lane == jnp.where(polar, 63, 31)) | (lane == jnp.where(polar, 95, 127))
+
+    def unpack(slot):
+        row = lax.rem(slot + 1, ROWS + 2)
         got_west, got_east = from_west[slot], from_east[slot]
-        for f in fields:
+        for f in range(NF):
             own = jnp.where(lane < 2, tile(row, f, 0), fixed(tile(row, f, 2), 30 - (LAST - 1)))
             halo = jnp.where(lane >= 96, fixed(got_west, 96 - 32 * f), fixed(got_east, 31 - 32 * f))
             value = jnp.where(lane < 31, own, halo)
-            if extra is not None and f != 1:
-                outer = roll(x_both[(0, None, 1, 2)[f]], 63 - extra)
-                value = jnp.where((lane == 63) | (lane == 95), outer, value)
+            if f != 1:
+                outer = roll(x_both[(0, None, 1, 2)[f]], jnp.where(polar, 63, 127) - slot)
+                value = jnp.where(outer_lanes, outer, value)
             edge[row, f] = value
 
     def late(r):
@@ -319,74 +373,85 @@
             more = gain * smooth[f * LEV : (f + 1) * LEV, 128:] + jnp.where(lane == LAST - 1, keep * last, 0.0)
             out[r, f, :, 256:COLS] = out[r, f, :, 256:COLS] + more[:, :LAST]
 
-    for i in range(GROUP):
-        early(1 + i)
-
-    @pl.when(first_north)
-    def _():
-        pl.semaphore_wait(ready.at[0], 1)
-        row_copy(0, north).start()
-
-    @pl.when(first_south)
-    def _():
-        pl.semaphore_wait(ready.at[1], 1)
-        row_copy(1, south).start()
-
     def early_group(g, carry):
         for i in range(GROUP):
-            early(g * GROUP + 1 + i)
+            early(lax.rem(g * GROUP + 1 + i, ROWS))
         return carry
 
-    lax.fori_loop(1, 3, early_group, 0)
-
-    @pl.when(has_north)
-    def _():
-        row_copy(1, north).wait_recv()
-
-    @pl.when(has_south)
-    def _():
-        row_copy(0, south).wait_recv()
-
-    for i, row in enumerate((0, ROWS + 1)):
-        to_east[ROWS + i], to_west[ROWS + i] = pack(row, (1, 2, 3))
+    def late_group(g, carry):
         for side in range(2):
-            corner_copy(i, side).start()
-    for r in (*range(3 * GROUP + 1, ROWS), 0):
-        early(r)
+
+            @pl.when(polar)
+            def _():
+                chunk_copy(2 * g + 1, side).wait()
+
+            @pl.when(polar & (g < ROWS // GROUP - 1))
+            def _():
+                chunk_copy(2 * g + 2, side).wait()
+
+            @pl.when(polar & (g == ROWS // GROUP - 1))
+            def _():
+                corner_copy(side).wait()
+
+        for i in range(GROUP):
+            unpack(g * GROUP + 2 + i)
+            late(lax.rem(g * GROUP + 1 + i, ROWS))
+        return carry
+
+    lax.fori_loop(0, 1, early_group, 0)
+
+    def outer_rows():
+        @pl.when(has_north)
+        def _():
+            row_copy(1, north).wait_recv()
+
+        @pl.when(has_south)
+        def _():
+            row_copy(0, south).wait_recv()
+
+        @pl.when(polar)
+        def _():
+            for i, row in enumerate((ROWS + 1, 0)):
+                to_east[ROWS + i], to_west[ROWS + i] = pack(row, (1, 2, 3))
+            for side in range(2):
+                corner_copy(side).start()
+
+    lax.fori_loop(1, 2, early_group, 0)
+    pl.when(~crossing)(outer_rows)
+    lax.fori_loop(2, jnp.where(crossing, 3, 4), early_group, 0)
+
+    @pl.when(last_south)
+    def _():
+        pl.semaphore_wait(ready.at[NORTH], 1)
+        row_copy(0, north).start()
+
+    @pl.when(first[SOUTH])
+    def _():
+        pl.semaphore_wait(ready.at[SOUTH], 1)
+        row_copy(1, south).start()
+
+
+    pl.when(crossing & polar)(outer_rows)
 
     for side in range(2):
         x_copy(side).wait()
+    near_x = jnp.where(polar, xf_east[...], xf_west[...])
+    far_x = jnp.where(polar, xf_west[...], xf_east[...])
     for slot in range(3):
-        x_both[slot] = jnp.where(lane < 32, fixed(xf_east[...], -32 * slot), fixed(xf_west[...], 32 - 32 * slot))
-
-    def arrived(c):
+        x_both[slot] = jnp.where(lane < 32, fixed(near_x, -32 * slot), fixed(far_x, 32 - 32 * slot))
+
+    @pl.when(polar)
+    def _():
         for side in range(2):
-            chunk_copy(c, side).wait()
-        for i in range(CHUNK):
-            unpack(c * CHUNK + i, c * CHUNK + i + 1, extra=c * CHUNK + i)
-
-    arrived(0)
-
-    def late_group(g, carry):
-        for i in range(GROUP // CHUNK):
-            for side in range(2):
-                chunk_copy(g * (GROUP // CHUNK) + 1 + i, side).wait()
-        for i in range(GROUP):
-            r = g * GROUP + CHUNK + i
-            unpack(r, r + 1, extra=r)
-        for i in range(GROUP):
-            late(g * GROUP + 1 + i)
-        return carry
-
-    lax.fori_loop(0, 3, late_group, 0)
-    for c in range(3 * GROUP // CHUNK + 1, NCHUNK):
-        arrived(c)
-    for i, row in enumerate((0, ROWS + 1)):
-        for side in range(2):
-            corner_copy(i, side).wait()
-        unpack(ROWS + i, row, (1, 2, 3))
-    for r in (*range(3 * GROUP + 1, ROWS), 0):
-        late(r)
+            chunk_copy(0, side).wait()
+
+    for slot in range(2):
+        unpack(slot)
+    lax.fori_loop(0, 1, late_group, 0)
+    lax.fori_loop(1, 3, late_group, 0)
+    pl.when(crossing & ~polar)(outer_rows)
+    lax.fori_loop(jnp.where(crossing, 3, 4), 4, early_group, 0)
+    lax.fori_loop(3, 4, late_group, 0)
 
     @pl.when(has_north)
     def _():
@@ -419,11 +484,10 @@
             pltpu.SMEM((256,), F32),
             pltpu.SMEM((8, 128), F32),
             dma((NCHUNK,)), dma((3,)),
-            dma((2, NCHUNK)), dma((2, NCHUNK)),
+            dma((2, NCHUNK + 1)), dma((2, NCHUNK + 1)),
             dma((2,)), dma((2,)),
             dma((2,)), dma((2,)),
-            dma((2, 2)), dma((2, 2)),
-            pltpu.SemaphoreType.REGULAR((2,)),
+            pltpu.SemaphoreType.REGULAR((4,)),
         ],
         compiler_params=pltpu.CompilerParams(
             collective_id=0, has_side_effects=True, vmem_limit_bytes=60 * 1024 * 1024

time: 16.1 us -> 14 us (0.87)
  the two profiles are of different devices: /device:TPU:38 before, /device:TPU:42 now
where the time goes in v3:
time: 14 us; the launch traced here: 13.9 us
  Pallas kernels  12.2 us (87%)
  local copies, waits for them, and re-layouts  1.67 us (12%)
    pallas_call x1, Pallas kernels, shards(): pl.pallas_call(kernel, out_shape=pltpu.VMEM(state.shape, F32), in_specs=[...  12.2 us
    unnamed x1, local copies, waits for them, and re-layouts  1.67 us

profile of v3, /device:TPU:42, one launch (start us, length us, event | category | flops | bytes accessed | tf_op | source)
XLA Modules:
  0.0 13.9 jit_solution(11283967182386079481)
XLA Ops:
  0.0 12.2 %shard_map.46 = f32[32,4,16,360]{3,2,1,0:T(8,128)S(1)} custom-call(f32[32,4,16,360]{3,2,1,0:T(8,128)} %state.1, s32[256]{0:T(256)} %band_hbm.1, f32[256]{0:T(256)} %damping_hbm.1, f32[16,8,128]{2,1,0:T(8,128)} %constant.2.clone.table_hbm), custom_call_target="tpu_custom_call" | custom-call | tf_op jit(solution)/shard_map/pallas_call | solution.py:470
  12.2 1.7 %copy.6 = f32[32,4,16,360]{3,2,1,0:T(8,128)} copy(f32[32,4,16,360]{3,2,1,0:T(8,128)S(1)} %shard_map.46) | data formatting | bytes 5898240

commit v4 on v3

--- a/solution.py
+++ b/solution.py
@@ -24,6 +24,7 @@
 LAST = COLS - 256
 CHUNK = 4
 NCHUNK = ROWS // CHUNK
+STAGES = (3, 5, 7, 8)
 GROUP = 8
 MESH = pl.DeviceIdType.MESH
 F32 = jnp.float32
@@ -200,11 +201,13 @@
                 xe = jnp.where(here, roll(tile(r + 1, f, 2), lax.rem(goal + 256 - jnp.where(polar, LAST - 33, LAST - 1), 128)), xe)
                 xw = jnp.where(here, roll(tile(r + 1, f, 0), lax.rem(goal + 256 - jnp.where(polar, 32, 0), 128)), xw)
 
-        @pl.when(polar & second[EAST])
+        early_chunk = polar & (c < STAGES[0])
+
+        @pl.when(early_chunk & second[EAST])
         def _():
             chunk_copy(c, 0).start()
 
-        @pl.when(polar & second[WEST])
+        @pl.when(early_chunk & second[WEST])
         def _():
             chunk_copy(c, 1).start()
 
@@ -214,27 +217,24 @@
     x_east[...] = xe
     x_west[...] = xw
 
-    def send_side(i):
-        pl.semaphore_wait(ready.at[(EAST, WEST)[i]], 1)
-
-        def send(c, carry):
-            chunk_copy(c, i).start()
-            return carry
-
-        lax.fori_loop(0, jnp.where(polar, NCHUNK, 0), send, 0)
-        x_copy(i).start()
-
-    @pl.when(second[EAST])
-    def _():
-        x_copy(0).start()
-
-    @pl.when(second[WEST])
-    def _():
-        x_copy(1).start()
+    def send_stage(stage):
+        ends = (0, *STAGES, NCHUNK)
+        for i in range(2):
+            is_first = first[(EAST, WEST)[i]]
+            begin = jnp.where(is_first, ends[stage - 1], ends[stage])
+            end = jnp.where(polar, jnp.where(is_first, ends[stage], ends[stage + 1]), begin)
+
+            def send(c, carry):
+                chunk_copy(c, i).start()
+                return carry
+
+            lax.fori_loop(begin, end, send, 0)
 
     @pl.when(first[EAST])
     def _():
-        send_side(0)
+        pl.semaphore_wait(ready.at[EAST], 1)
+
+    x_copy(0).start()
 
     @pl.when(first[NORTH] & ~last_south)
     def _():
@@ -243,8 +243,10 @@
 
     @pl.when(first[WEST])
     def _():
-        send_side(1)
-
+        pl.semaphore_wait(ready.at[WEST], 1)
+
+    x_copy(1).start()
+    send_stage(1)
     for copy in smalls:
         copy.wait()
 
@@ -379,27 +381,17 @@
         return carry
 
     def late_group(g, carry):
-        for side in range(2):
-
-            @pl.when(polar)
-            def _():
+        @pl.when(polar)
+        def _():
+            for side in range(2):
                 chunk_copy(2 * g + 1, side).wait()
-
-            @pl.when(polar & (g < ROWS // GROUP - 1))
-            def _():
                 chunk_copy(2 * g + 2, side).wait()
-
-            @pl.when(polar & (g == ROWS // GROUP - 1))
-            def _():
-                corner_copy(side).wait()
 
         for i in range(GROUP):
             unpack(g * GROUP + 2 + i)
             late(lax.rem(g * GROUP + 1 + i, ROWS))
         return carry
 
-    lax.fori_loop(0, 1, early_group, 0)
-
     def outer_rows():
         @pl.when(has_north)
         def _():
@@ -416,10 +408,17 @@
             for side in range(2):
                 corner_copy(side).start()
 
+    def outer_early():
+        for r in (ROWS - 1, 0):
+            early(r)
+
+    lax.fori_loop(0, 1, early_group, 0)
+    send_stage(2)
     lax.fori_loop(1, 2, early_group, 0)
-    pl.when(~crossing)(outer_rows)
-    lax.fori_loop(2, jnp.where(crossing, 3, 4), early_group, 0)
-
+    send_stage(3)
+    pl.when(~crossing & polar)(outer_rows)
+    lax.fori_loop(2, 3, early_group, 0)
+    send_stage(4)
     @pl.when(last_south)
     def _():
         pl.semaphore_wait(ready.at[NORTH], 1)
@@ -431,7 +430,11 @@
         row_copy(1, south).start()
 
 
+    for r in range(3 * GROUP + 1, ROWS - 1):
+        early(r)
+
     pl.when(crossing & polar)(outer_rows)
+    pl.when(polar)(outer_early)
 
     for side in range(2):
         x_copy(side).wait()
@@ -447,11 +450,31 @@
 
     for slot in range(2):
         unpack(slot)
-    lax.fori_loop(0, 1, late_group, 0)
-    lax.fori_loop(1, 3, late_group, 0)
-    pl.when(crossing & ~polar)(outer_rows)
-    lax.fori_loop(jnp.where(crossing, 3, 4), 4, early_group, 0)
-    lax.fori_loop(3, 4, late_group, 0)
+    lax.fori_loop(0, 3, late_group, 0)
+
+    @pl.when(polar)
+    def _():
+        for side in range(2):
+            chunk_copy(NCHUNK - 1, side).wait()
+
+    for r in range(3 * GROUP + 1, ROWS - 1):
+        unpack(r + 1)
+        late(r)
+
+    @pl.when(~polar)
+    def _():
+        outer_rows()
+        outer_early()
+
+    @pl.when(polar)
+    def _():
+        for side in range(2):
+            corner_copy(side).wait()
+
+    unpack(ROWS)
+    unpack(ROWS + 1)
+    late(ROWS - 1)
+    late(0)
 
     @pl.when(has_north)
     def _():

time: 14 us -> 13.3 us (0.950)
  the two profiles are of different devices: /device:TPU:42 before, /device:TPU:32 now
where the time goes in v4:
time: 13.3 us; the launch traced here: 13.2 us
  Pallas kernels  11.5 us (86%)
  local copies, waits for them, and re-layouts  1.67 us (13%)
    pallas_call x1, Pallas kernels, shards(): pl.pallas_call(kernel, out_shape=pltpu.VMEM(state.shape, F32), in_specs=[...  11.5 us
    unnamed x1, local copies, waits for them, and re-layouts  1.67 us

profile of v4, /device:TPU:32, one launch (start us, length us, event | category | flops | bytes accessed | tf_op | source)
XLA Modules:
  0.0 13.2 jit_solution(7821069856416138154)
XLA Ops:
  0.0 11.5 %shard_map.46 = f32[32,4,16,360]{3,2,1,0:T(8,128)S(1)} custom-call(f32[32,4,16,360]{3,2,1,0:T(8,128)} %state.1, s32[256]{0:T(256)} %band_hbm.1, f32[256]{0:T(256)} %damping_hbm.1, f32[16,8,128]{2,1,0:T(8,128)} %constant.2.clone.table_hbm), custom_call_target="tpu_custom_call" | custom-call | tf_op jit(solution)/shard_map/pallas_call | solution.py:493
  11.5 1.7 %copy.6 = f32[32,4,16,360]{3,2,1,0:T(8,128)} copy(f32[32,4,16,360]{3,2,1,0:T(8,128)S(1)} %shard_map.46) | data formatting | bytes 5898240

commit v5 on v4

--- a/solution.py
+++ b/solution.py
@@ -408,6 +408,19 @@
             for side in range(2):
                 corner_copy(side).start()
 
+    def crossing_send():
+        @pl.when(last_south)
+        def _():
+            pl.semaphore_wait(ready.at[NORTH], 1)
+            row_copy(0, north).start()
+
+        @pl.when(first[SOUTH])
+        def _():
+            pl.semaphore_wait(ready.at[SOUTH], 1)
+            row_copy(1, south).start()
+
+    soon = polar & ~crossing & (lon == NLON_DEV - 1)
+
     def outer_early():
         for r in (ROWS - 1, 0):
             early(r)
@@ -416,24 +429,16 @@
     send_stage(2)
     lax.fori_loop(1, 2, early_group, 0)
     send_stage(3)
-    pl.when(~crossing & polar)(outer_rows)
+    pl.when(soon)(outer_rows)
+    pl.when(lon < 2)(crossing_send)
     lax.fori_loop(2, 3, early_group, 0)
     send_stage(4)
-    @pl.when(last_south)
-    def _():
-        pl.semaphore_wait(ready.at[NORTH], 1)
-        row_copy(0, north).start()
-
-    @pl.when(first[SOUTH])
-    def _():
-        pl.semaphore_wait(ready.at[SOUTH], 1)
-        row_copy(1, south).start()
-
+    pl.when(lon >= 2)(crossing_send)
 
     for r in range(3 * GROUP + 1, ROWS - 1):
         early(r)
 
-    pl.when(crossing & polar)(outer_rows)
+    pl.when(polar & ~soon)(outer_rows)
     pl.when(polar)(outer_early)
 
     for side in range(2):

time: 13.3 us -> 13.1 us (0.985)
  Pallas kernels: 11.5 us -> 11.3 us
    pallas_call x1, Pallas kernels: 11.5 us -> 11.3 us  [shards(): pl.pallas_call(kernel, out_shape=pltpu.VMEM(state.shape, F32), in_specs=[...]
where the time goes in v5:
time: 13.1 us; the launch traced here: 13 us
  Pallas kernels  11.3 us (86%)
  local copies, waits for them, and re-layouts  1.67 us (13%)
    pallas_call x1, Pallas kernels, shards(): pl.pallas_call(kernel, out_shape=pltpu.VMEM(state.shape, F32), in_specs=[...  11.3 us
    unnamed x1, local copies, waits for them, and re-layouts  1.67 us

profile of v5, /device:TPU:32, one launch (start us, length us, event | category | flops | bytes accessed | tf_op | source)
XLA Modules:
  0.0 13.0 jit_solution(15208259671996434127)
XLA Ops:
  0.0 11.3 %shard_map.46 = f32[32,4,16,360]{3,2,1,0:T(8,128)S(1)} custom-call(f32[32,4,16,360]{3,2,1,0:T(8,128)} %state.1, s32[256]{0:T(256)} %band_hbm.1, f32[256]{0:T(256)} %damping_hbm.1, f32[16,8,128]{2,1,0:T(8,128)} %constant.2.clone.table_hbm), custom_call_target="tpu_custom_call" | custom-call | tf_op jit(solution)/shard_map/pallas_call | solution.py:498
  11.3 1.7 %copy.6 = f32[32,4,16,360]{3,2,1,0:T(8,128)} copy(f32[32,4,16,360]{3,2,1,0:T(8,128)S(1)} %shard_map.46) | data formatting | bytes 5898240

commit v6 on v5

--- a/solution.py
+++ b/solution.py
@@ -427,19 +427,24 @@
 
     lax.fori_loop(0, 1, early_group, 0)
     send_stage(2)
+    pl.when(lon < 2)(crossing_send)
     lax.fori_loop(1, 2, early_group, 0)
     send_stage(3)
     pl.when(soon)(outer_rows)
-    pl.when(lon < 2)(crossing_send)
+    pl.when(lon >= 2)(crossing_send)
     lax.fori_loop(2, 3, early_group, 0)
     send_stage(4)
-    pl.when(lon >= 2)(crossing_send)
 
     for r in range(3 * GROUP + 1, ROWS - 1):
         early(r)
 
-    pl.when(polar & ~soon)(outer_rows)
-    pl.when(polar)(outer_early)
+    patient = crossing & (lon < NLON_DEV - 1)
+
+    @pl.when(polar & ~patient)
+    def _():
+        pl.when(~soon)(outer_rows)
+        outer_early()
+
 
     for side in range(2):
         x_copy(side).wait()
@@ -455,7 +460,14 @@
 
     for slot in range(2):
         unpack(slot)
-    lax.fori_loop(0, 3, late_group, 0)
+    lax.fori_loop(0, 1, late_group, 0)
+
+    @pl.when(polar & patient)
+    def _():
+        outer_rows()
+        outer_early()
+
+    lax.fori_loop(1, 3, late_group, 0)
 
     @pl.when(polar)
     def _():

time: 13.1 us -> 13.1 us (level)
  no operation moved by 1% of the time
where the time goes in v6:
time: 13.1 us; the launch traced here: 13 us
  Pallas kernels  11.3 us (86%)
  local copies, waits for them, and re-layouts  1.67 us (13%)
    pallas_call x1, Pallas kernels, shards(): pl.pallas_call(kernel, out_shape=pltpu.VMEM(state.shape, F32), in_specs=[...  11.3 us
    unnamed x1, local copies, waits for them, and re-layouts  1.67 us

profile of v6, /device:TPU:32, one launch (start us, length us, event | category | flops | bytes accessed | tf_op | source)
XLA Modules:
  0.0 13.0 jit_solution(14866510064971222590)
XLA Ops:
  0.0 11.3 %shard_map.46 = f32[32,4,16,360]{3,2,1,0:T(8,128)S(1)} custom-call(f32[32,4,16,360]{3,2,1,0:T(8,128)} %state.1, s32[256]{0:T(256)} %band_hbm.1, f32[256]{0:T(256)} %damping_hbm.1, f32[16,8,128]{2,1,0:T(8,128)} %constant.2.clone.table_hbm), custom_call_target="tpu_custom_call" | custom-call | tf_op jit(solution)/shard_map/pallas_call | solution.py:510
  11.3 1.7 %copy.6 = f32[32,4,16,360]{3,2,1,0:T(8,128)} copy(f32[32,4,16,360]{3,2,1,0:T(8,128)S(1)} %shard_map.46) | data formatting | bytes 5898240

commit v7 on v6

--- a/solution.py
+++ b/solution.py
@@ -284,7 +284,7 @@
     def product(left, right):
         return jnp.dot(left, right, preferred_element_type=F32)
 
-    def early(r):
+    def early(r, filtered=True):
         row = r + 1
         width, keep, gain = coefficients(r)
         mids = [[tile(row, f, t) for t in range(3)] for f in range(NF)]
@@ -313,6 +313,14 @@
             if t == 2:
                 values = [jnp.where(lane >= LAST - 1, 0.0, a) for a in values]
             stepped.append(values)
+        if not filtered:
+            for t in range(3):
+                for f in range(NF):
+                    if t < 2:
+                        out[r, f, :, t * 128 : (t + 1) * 128] = stepped[t][f]
+                    else:
+                        out[r, f, :, 256:COLS] = stepped[t][f][:, :LAST]
+            return
         right = weights(near, width)
         parts = [[halves(a) for a in values] for values in stepped]
         zero = jnp.zeros((LEV, 128), BF16)
@@ -352,7 +360,7 @@
                 value = jnp.where(outer_lanes, outer, value)
             edge[row, f] = value
 
-    def late(r):
+    def late(r, filtered=True):
         row = r + 1
         width, keep, gain = coefficients(r)
 
@@ -364,6 +372,12 @@
             r, lambda f: mids[f], lambda f: edge[row + 1, f], lambda f: edge[row - 1, f],
             (difference(mids[0] * mids[2]), difference(mids[2]), difference(mids[3])),
         )
+        if not filtered:
+            for f in range(NF):
+                out[r, f, :, 0:128] = jnp.where(lane == 0, stepped[f], out[r, f, :, 0:128])
+                last = roll(stepped[f], LAST - 1 - 30)[:, :LAST]
+                out[r, f, :, 256:COLS] = jnp.where(lane[:, :LAST] == LAST - 1, last, out[r, f, :, 256:COLS])
+            return
         right = weights(far, width)
         parts = [halves(a) for a in stepped]
         left = jnp.concatenate([jnp.concatenate(p, axis=1) for p in parts], axis=0)
@@ -478,20 +492,24 @@
         unpack(r + 1)
         late(r)
 
+    def outer_late(filtered):
+        unpack(ROWS)
+        unpack(ROWS + 1)
+        late(ROWS - 1, filtered)
+        late(0, filtered)
+
     @pl.when(~polar)
     def _():
         outer_rows()
-        outer_early()
+        for r in (ROWS - 1, 0):
+            early(r, False)
+        outer_late(False)
 
     @pl.when(polar)
     def _():
         for side in range(2):
             corner_copy(side).wait()
-
-    unpack(ROWS)
-    unpack(ROWS + 1)
-    late(ROWS - 1)
-    late(0)
+        outer_late(True)
 
     @pl.when(has_north)
     def _():

time: 13.1 us -> 12.7 us (0.969)
  Pallas kernels: 11.3 us -> 10.9 us
    pallas_call x1, Pallas kernels: 11.3 us -> 10.9 us  [shards(): pl.pallas_call(kernel, out_shape=pltpu.VMEM(state.shape, F32), in_specs=[...]
where the time goes in v7:
time: 12.7 us; the launch traced here: 12.6 us
  Pallas kernels  10.9 us (86%)
  local copies, waits for them, and re-layouts  1.67 us (13%)
    pallas_call x1, Pallas kernels, shards(): pl.pallas_call(kernel, out_shape=pltpu.VMEM(state.shape, F32), in_specs=[...  10.9 us
    unnamed x1, local copies, waits for them, and re-layouts  1.67 us

profile of v7, /device:TPU:32, one launch (start us, length us, event | category | flops | bytes accessed | tf_op | source)
XLA Modules:
  0.0 12.6 jit_solution(10498448765317921962)
XLA Ops:
  0.0 10.9 %shard_map.46 = f32[32,4,16,360]{3,2,1,0:T(8,128)S(1)} custom-call(f32[32,4,16,360]{3,2,1,0:T(8,128)} %state.1, s32[256]{0:T(256)} %band_hbm.1, f32[256]{0:T(256)} %damping_hbm.1, f32[16,8,128]{2,1,0:T(8,128)} %constant.2.clone.table_hbm), custom_call_target="tpu_custom_call" | custom-call | tf_op jit(solution)/shard_map/pallas_call | solution.py:528
  10.9 1.7 %copy.6 = f32[32,4,16,360]{3,2,1,0:T(8,128)} copy(f32[32,4,16,360]{3,2,1,0:T(8,128)S(1)} %shard_map.46) | data formatting | bytes 5898240
